TPU v7x, 32 devices: a whole 2x2x4 slice. The times are simulated.
32 devices in a mesh: space: 8 (over z, y), param: 4 (over x, core).
Axes of the slice: x: 2, y: 2, z: 4, core: 2. Of those that a mesh axis runs over, the one named last changes fastest.
Arguments:
- snapshots: float32 [49152, 4096], P('space', 'param'), may hold values from -1800 to 1800
- sketch: float32 [4096, 32], P('param'), may hold values from -0.09375 to 0.09375
- sketch_next: float32 [256, 32], replicated, may hold values from -0.375 to 0.375
Outputs:
- first_core: float32 [32, 49152], P(None, 'space')
- second_core: float32 [32, 512], P(None, 'param')
- remainder: float32 [32, 256], replicated
All inputs are finite; a program needn't handle non-finite values.
Results may differ from a plain program's by a relative error of at most 0.00016.
Values sent between devices are 32-bit elements; how exact they have to be, the bound alone decides.
No kernel may reach another device: no remote copies, remote signals or barrier semaphores. Data moves between devices by JAX's collectives and lax.ppermute only.
A program may use at most 128 MiB of HBM per device.

v0:
```python
import math

import jax
import jax.numpy as jnp
from jax import lax
from jax.sharding import PartitionSpec as P

R = 32
N2 = 16
N3 = 16
ITERS = 3


def gram_matrix(block):
    return jnp.dot(block, block.T, precision=lax.Precision.HIGHEST)


def apply_factor(lower, block):
    return jax.scipy.linalg.solve_triangular(lower, block, lower=True)


def frame_space(block):
    lower = jnp.linalg.cholesky(lax.psum(gram_matrix(block), "space"))
    return apply_factor(lower, block)


def frame_param(block):
    lower = jnp.linalg.cholesky(lax.psum(gram_matrix(block), "param"))
    return apply_factor(lower, block)


def shards(snapshots, sketch, sketch_next):
    highest = lax.Precision.HIGHEST
    rows_total = snapshots.shape[0] * lax.axis_size("space")

    def new_basis(partial_value):
        return frame_space(lax.psum(partial_value, "param"))

    def project(basis):
        return lax.psum(jnp.dot(basis, snapshots, precision=highest), "space")

    partial_value = lax.dot_general(sketch, snapshots, (((0,), (1,)), ((), ())), precision=highest)
    basis = new_basis(partial_value)
    for step in range(ITERS):
        column_frame = frame_param(project(basis))
        partial_value = lax.dot_general(
            column_frame, snapshots, (((1,), (1,)), ((), ())), precision=highest
        )
        basis = new_basis(partial_value)
    coefficients = project(basis) / math.sqrt(rows_total)
    local_modes = coefficients.shape[1] // (N2 * N3)
    unfold = (
        coefficients.reshape(R, local_modes, N2 * N3)
        .transpose(1, 0, 2)
        .reshape(local_modes * R, N2 * N3)
    )
    second_sketch = lax.dot_general(
        sketch_next, unfold, (((0,), (1,)), ((), ())), precision=highest
    )
    second_frame = frame_param(second_sketch)
    next_rows = unfold.shape[0] * lax.axis_size("param")
    summed = lax.psum(jnp.dot(second_frame, unfold, precision=highest), "param")
    return (
        basis * math.sqrt(rows_total),
        second_frame * math.sqrt(next_rows),
        summed / math.sqrt(next_rows),
    )


def solution(mesh):
    placed = (P("space", "param"), P("param", None), P())
    return jax.shard_map(
        shards,
        mesh=mesh,
        in_specs=placed,
        out_specs=(P(None, "space"), P(None, "param"), P()),
        check_vma=False,
    )
```

profile of v0, /device:TPU:0, one launch (start us, length us, event | category | flops | bytes accessed | tf_op | source)
XLA Modules:
  0.0 880.0 jit_solution(3580967928332802097)
XLA Ops:
  8.1 26.3 %fusion.44 = f32[32,6144]{1,0:T(8,128)} fusion(f32[1024,32]{0,1:T(8,128)S(1)} %copy-done, f32[6144,1024]{1,0:T(8,128)} %param.8), kind=kOutput, calls=%fused_computation.77 | convolution fusion | flops 2415919104 | bytes 26083328 | tf_op jit(solution)/shard_map/dot_general | solution.py:42
  34.5 37.4 %all-reduce.9.cloned.1.call-done = f32[32,6144]{1,0:T(8,128)} async-done(((f32[32,6144]{1,0:T(8,128)}), f32[32,6144]{1,0:T(8,128)}) %all-reduce.9.cloned.1.call-update) | async-done | bytes 786448 | tf_op jit(solution)/shard_map/psum | solution.py:37
  71.9 2.1 fusion.45
  74.0 37.1 %psum.120 = f32[32,32]{0,1:T(8,128)S(1)} all-reduce(f32[32,32]{0,1:T(8,128)S(1)} %fusion.45), channel_id=1, replica_groups=mesh['space'=8,'param'=4] {'space'}, use_global_device_ids=true, to_apply=%region_1.0 | all-reduce | flops 1024 | bytes 8192 | tf_op jit(solution)/shard_map/psum | solution.py:23
  111.2 2.9 cholesky.134
  115.5 2.4 custom-call.18
  117.9 2.0 fusion.29
  119.9 18.1 %fusion.46 = f32[32,1024]{1,0:T(8,128)} fusion(f32[32,6144]{1,0:T(8,128)S(1)} %fusion.29, f32[6144,1024]{1,0:T(8,128)} %param.8), kind=kOutput, calls=%fused_computation.79 | convolution fusion | flops 2415919104 | bytes 26083328 | tf_op jit(solution)/shard_map/dot_general | solution.py:40
  138.1 66.1 %all-reduce.11.cloned.1.call-done = f32[32,1024]{1,0:T(8,128)} async-done(((f32[32,1024]{1,0:T(8,128)}), f32[32,1024]{1,0:T(8,128)}) %all-reduce.11.cloned.1.call-update) | async-done | bytes 131088 | tf_op jit(solution)/shard_map/psum | solution.py:40
  205.4 10.3 %psum.122 = f32[32,32]{0,1:T(8,128)S(1)} all-reduce(f32[32,32]{0,1:T(8,128)S(1)} %fusion.47), channel_id=1, replica_groups=mesh['space'=8,'param'=4] {'param'}, use_global_device_ids=true, to_apply=%region_5.8 | all-reduce | flops 1024 | bytes 8192 | tf_op jit(solution)/shard_map/psum | solution.py:28
  215.8 2.9 cholesky.145
  220.1 2.4 custom-call.19
  223.7 26.3 %fusion.48 = f32[32,6144]{1,0:T(8,128)} fusion(f32[32,1024]{1,0:T(8,128)S(1)} %fusion.26, f32[6144,1024]{1,0:T(8,128)} %param.8), kind=kOutput, calls=%fused_computation.81 | convolution fusion | flops 2415919104 | bytes 26083328 | tf_op jit(solution)/shard_map/dot_general | solution.py:46
  250.1 34.2 %all-reduce.13.cloned.1.call-done = f32[32,6144]{1,0:T(8,128)} async-done(((f32[32,6144]{1,0:T(8,128)}), f32[32,6144]{1,0:T(8,128)}) %all-reduce.13.cloned.1.call-update) | async-done | bytes 786448 | tf_op jit(solution)/shard_map/psum | solution.py:37
  284.3 2.1 fusion.49
  286.5 37.1 %psum.124 = f32[32,32]{0,1:T(8,128)S(1)} all-reduce(f32[32,32]{0,1:T(8,128)S(1)} %fusion.49), channel_id=1, replica_groups=mesh['space'=8,'param'=4] {'space'}, use_global_device_ids=true, to_apply=%region_7.0 | all-reduce | flops 1024 | bytes 8192 | tf_op jit(solution)/shard_map/psum | solution.py:23
  323.6 2.9 cholesky.156
  327.9 2.4 custom-call.20
  330.3 2.0 fusion.23
  332.3 18.1 %fusion.50 = f32[32,1024]{1,0:T(8,128)} fusion(f32[32,6144]{1,0:T(8,128)S(1)} %fusion.23, f32[6144,1024]{1,0:T(8,128)} %param.8), kind=kOutput, calls=%fused_computation.83 | convolution fusion | flops 2415919104 | bytes 26083328 | tf_op jit(solution)/shard_map/dot_general | solution.py:40
  350.5 66.1 %all-reduce.15.cloned.1.call-done = f32[32,1024]{1,0:T(8,128)} async-done(((f32[32,1024]{1,0:T(8,128)}), f32[32,1024]{1,0:T(8,128)}) %all-reduce.15.cloned.1.call-update) | async-done | bytes 131088 | tf_op jit(solution)/shard_map/psum | solution.py:40
  417.9 10.3 %psum.126 = f32[32,32]{0,1:T(8,128)S(1)} all-reduce(f32[32,32]{0,1:T(8,128)S(1)} %fusion.51), channel_id=1, replica_groups=mesh['space'=8,'param'=4] {'param'}, use_global_device_ids=true, to_apply=%region_9.0 | all-reduce | flops 1024 | bytes 8192 | tf_op jit(solution)/shard_map/psum | solution.py:28
  428.3 2.9 cholesky.167
  432.5 2.4 custom-call.21
  436.2 26.3 %fusion.52 = f32[32,6144]{1,0:T(8,128)} fusion(f32[32,1024]{1,0:T(8,128)S(1)} %fusion.20, f32[6144,1024]{1,0:T(8,128)} %param.8), kind=kOutput, calls=%fused_computation.85 | convolution fusion | flops 2415919104 | bytes 26083328 | tf_op jit(solution)/shard_map/dot_general | solution.py:46
  462.6 34.2 %all-reduce.17.cloned.1.call-done = f32[32,6144]{1,0:T(8,128)} async-done(((f32[32,6144]{1,0:T(8,128)}), f32[32,6144]{1,0:T(8,128)}) %all-reduce.17.cloned.1.call-update) | async-done | bytes 786448 | tf_op jit(solution)/shard_map/psum | solution.py:37
  496.8 2.1 fusion.53
  499.0 37.1 %psum.128 = f32[32,32]{0,1:T(8,128)S(1)} all-reduce(f32[32,32]{0,1:T(8,128)S(1)} %fusion.53), channel_id=1, replica_groups=mesh['space'=8,'param'=4] {'space'}, use_global_device_ids=true, to_apply=%region_11.0 | all-reduce | flops 1024 | bytes 8192 | tf_op jit(solution)/shard_map/psum | solution.py:23
  536.1 2.9 cholesky.178
  540.4 2.4 custom-call.22
  544.8 18.1 %fusion.54 = f32[32,1024]{1,0:T(8,128)} fusion(f32[32,6144]{1,0:T(8,128)S(1)} %fusion.17, f32[6144,1024]{1,0:T(8,128)} %param.8), kind=kOutput, calls=%fused_computation.87 | convolution fusion | flops 2415919104 | bytes 26083328 | tf_op jit(solution)/shard_map/dot_general | solution.py:40
  563.0 66.1 %all-reduce.19.cloned.1.call-done = f32[32,1024]{1,0:T(8,128)} async-done(((f32[32,1024]{1,0:T(8,128)}), f32[32,1024]{1,0:T(8,128)}) %all-reduce.19.cloned.1.call-update) | async-done | bytes 131088 | tf_op jit(solution)/shard_map/psum | solution.py:40
  630.3 10.4 %psum.130 = f32[32,32]{0,1:T(8,128)S(1)} all-reduce(f32[32,32]{0,1:T(8,128)S(1)} %fusion.55), channel_id=1, replica_groups=mesh['space'=8,'param'=4] {'param'}, use_global_device_ids=true, to_apply=%region_13.0 | all-reduce | flops 1024 | bytes 8192 | tf_op jit(solution)/shard_map/psum | solution.py:28
  640.8 2.9 cholesky.189
  645.1 2.4 custom-call.23
  648.8 26.3 %fusion.56 = f32[32,6144]{1,0:T(8,128)} fusion(f32[32,1024]{1,0:T(8,128)S(1)} %fusion.14, f32[6144,1024]{1,0:T(8,128)} %param.8), kind=kOutput, calls=%fused_computation.89 | convolution fusion | flops 2415919104 | bytes 26083328 | tf_op jit(solution)/shard_map/dot_general | solution.py:46
  675.1 34.2 %all-reduce.21.cloned.1.call-done = f32[32,6144]{1,0:T(8,128)} async-done(((f32[32,6144]{1,0:T(8,128)}), f32[32,6144]{1,0:T(8,128)}) %all-reduce.21.cloned.1.call-update) | async-done | bytes 786448 | tf_op jit(solution)/shard_map/psum | solution.py:37
  709.4 2.1 fusion.57
  711.5 37.1 %psum.132 = f32[32,32]{0,1:T(8,128)S(1)} all-reduce(f32[32,32]{0,1:T(8,128)S(1)} %fusion.57), channel_id=1, replica_groups=mesh['space'=8,'param'=4] {'space'}, use_global_device_ids=true, to_apply=%region_15.0 | all-reduce | flops 1024 | bytes 8192 | tf_op jit(solution)/shard_map/psum | solution.py:23
  748.7 2.9 cholesky.200
  752.9 2.4 custom-call.24
  755.4 2.9 broadcast_multiply_fusion
  758.2 18.1 %fusion.58 = f32[32,1024]{1,0:T(8,128)} fusion(f32[32,6144]{1,0:T(8,128)S(1)} %get-tuple-element.7, f32[6144,1024]{1,0:T(8,128)} %param.8), kind=kOutput, calls=%fused_computation.91 | convolution fusion | flops 2415919104 | bytes 26083328 | tf_op jit(solution)/shard_map/dot_general | solution.py:40
  776.4 66.1 %all-reduce.23.cloned.1.call-done = f32[32,1024]{1,0:T(8,128)} async-done(((f32[32,1024]{1,0:T(8,128)}), f32[32,1024]{1,0:T(8,128)}) %all-reduce.23.cloned.1.call-update) | async-done | bytes 131088 | tf_op jit(solution)/shard_map/psum | solution.py:40
  843.9 10.1 %psum.134 = f32[32,32]{0,1:T(8,128)S(1)} all-reduce(f32[32,32]{0,1:T(8,128)S(1)} %fusion.60), channel_id=1, replica_groups=mesh['space'=8,'param'=4] {'param'}, use_global_device_ids=true, to_apply=%region_17.21 | all-reduce | flops 1024 | bytes 8192 | tf_op jit(solution)/shard_map/psum | solution.py:28
  854.1 2.9 cholesky.211
  858.3 2.4 custom-call.12
  861.8 10.3 %psum.135 = f32[32,256]{1,0:T(8,128)S(1)} all-reduce(f32[32,256]{1,0:T(8,128)S(1)} %fusion.61), channel_id=1, replica_groups=mesh['space'=8,'param'=4] {'param'}, use_global_device_ids=true, to_apply=%region_18.22 | all-reduce | flops 8192 | bytes 65536 | tf_op jit(solution)/shard_map/psum | solution.py:62
  (74 shorter events, 24.9 us)
Async XLA Ops:
  7.2 0.9 copy-start
  7.2 64.7 %all-reduce.9.cloned.1.call-start = ((), (), s32[]{:S(2)}) async-start(), calls=%async_computation | async-start | bytes 1572864 | tf_op jit(solution)/shard_map/psum | solution.py:37
  34.4 169.8 %all-reduce.11.cloned.1.call-start = ((), (), s32[]{:S(2)}) async-start(), calls=%async_computation.1 | async-start | bytes 262144 | tf_op jit(solution)/shard_map/psum | solution.py:40
  138.0 146.3 %all-reduce.13.cloned.1.call-start = ((), (), s32[]{:S(2)}) async-start(), calls=%async_computation.2 | async-start | bytes 1572864 | tf_op jit(solution)/shard_map/psum | solution.py:37
  250.1 166.5 %all-reduce.15.cloned.1.call-start = ((), (), s32[]{:S(2)}) async-start(), calls=%async_computation.3 | async-start | bytes 262144 | tf_op jit(solution)/shard_map/psum | solution.py:40
  350.5 146.3 %all-reduce.17.cloned.1.call-start = ((), (), s32[]{:S(2)}) async-start(), calls=%async_computation.4 | async-start | bytes 1572864 | tf_op jit(solution)/shard_map/psum | solution.py:37
  462.6 166.6 %all-reduce.19.cloned.1.call-start = ((), (), s32[]{:S(2)}) async-start(), calls=%async_computation.5 | async-start | bytes 262144 | tf_op jit(solution)/shard_map/psum | solution.py:40
  563.0 146.4 %all-reduce.21.cloned.1.call-start = ((), (), s32[]{:S(2)}) async-start(), calls=%async_computation.6 | async-start | bytes 1572864 | tf_op jit(solution)/shard_map/psum | solution.py:37
  648.7 194.7 %copy-start.1 = (f32[256,32]{0,1:T(8,128)S(1)}, f32[256,32]{0,1:T(8,128)}, u32[]{:S(2)}) copy-start(f32[256,32]{0,1:T(8,128)} %param.10) | copy-start | bytes 98308
  675.1 167.4 %all-reduce.23.cloned.1.call-start = ((), (), s32[]{:S(2)}) async-start(), calls=%async_computation.7 | async-start | bytes 262144 | tf_op jit(solution)/shard_map/psum | solution.py:40
Sparse Core Ops, SparseCore 0:
  34.5 37.3 all-reduce.8
  138.2 65.9 all-reduce.10
  250.2 34.0 all-reduce.12
  350.6 65.9 all-reduce.14
  462.7 34.0 all-reduce.16
  563.1 65.9 all-reduce.18
  675.2 34.1 all-reduce.20
  776.5 65.9 all-reduce.22
where the time goes:
time: 888 us; the launch traced here: 880 us
  waiting for transfers between devices  405 us (46%)
  matrix products  204 us (23%)
  blocking collectives  200 us (23%)
  other arithmetic  55 us (6%)
  between operations  14.8 us (2%)
    psum x4, waiting for transfers between devices, project(): return lax.psum(jnp.dot(basis, snapshots, precision=highest), 'space')  264 us
    psum x4, blocking collectives, frame_space(): lower = jnp.linalg.cholesky(lax.psum(gram_matrix(block), 'space'))  148 us
    psum x4, waiting for transfers between devices, new_basis(): return frame_space(lax.psum(partial_value, 'param'))  140 us
    dot_general x3, matrix products, shards(): lax.dot_general(column_frame, snapshots, (((1,), (1,)), ((), ())), precis...  79 us
    dot_general x4, matrix products, project(): return lax.psum(jnp.dot(basis, snapshots, precision=highest), 'space')  72.6 us
    psum x4, blocking collectives, frame_param(): lower = jnp.linalg.cholesky(lax.psum(gram_matrix(block), 'param'))  41.1 us
    dot_general x1, matrix products, shards(): lax.dot_general(sketch, snapshots, (((0,), (1,)), ((), ())), precision=hi...  26.3 us
    another operation x16, other arithmetic, apply_factor(): return jax.scipy.linalg.solve_triangular(lower, block, lower=True)  24.7 us
  transfers between devices with their start and end apart: 8, of which 8 were waited for; matrix products, arithmetic and copies ran while one was open for 0% of the time, Pallas kernels for 0%

commit v1 on v0

v1 whole, which is shorter than its diff:
```python
import math

import jax
import jax.numpy as jnp
from jax import lax
from jax.experimental import pallas as pl
from jax.experimental.pallas import tpu as pltpu
from jax.sharding import PartitionSpec as P

R = 32
N2 = 16
N3 = 16
ITERS = 3
HIGHEST = lax.Precision.HIGHEST
F32 = jnp.float32
BF16 = jnp.bfloat16
LANES = 128
NT = (((1,), (1,)), ((), ()))


def split(block):
    high = block.astype(BF16)
    return high, (block - high.astype(F32)).astype(BF16)


def rows_kernel(frame_ref, a_ref, out_ref):
    frame_high, frame_low = split(frame_ref[...])
    both = jnp.concatenate([frame_high, frame_low], axis=0)
    high, low = split(a_ref[...])
    first = lax.dot_general(both, high, NT, preferred_element_type=F32)
    second = lax.dot_general(frame_high, low, NT, preferred_element_type=F32)
    out_ref[...] = first[:R] + (first[R:] + second)


def columns_kernel(s_ref, a_ref, out_ref):
    s = s_ref[...]
    s_high, s_low = split(s)
    both = jnp.concatenate([s_high, s_low], axis=0)
    high, low = split(a_ref[...])
    first = jnp.dot(both, high, preferred_element_type=F32)
    second = jnp.dot(s_high, low, preferred_element_type=F32)
    product = first[:R] + (first[R:] + second)
    gram = lax.dot_general(s, s, NT, precision=HIGHEST, preferred_element_type=F32)
    gram = jnp.concatenate([gram, jnp.zeros((R, LANES - R), F32)], axis=1)
    whole = jnp.concatenate([product, gram], axis=1)

    @pl.when(pl.program_id(0) == 0)
    def _():
        out_ref[...] = whole

    @pl.when(pl.program_id(0) > 0)
    def _():
        out_ref[...] += whole


def inverse_factor(gram):
    rows = lax.broadcasted_iota(jnp.int32, (R, LANES), 0)
    lanes = lax.broadcasted_iota(jnp.int32, (R, LANES), 1)
    state = gram + jnp.where(lanes == rows + R, 1.0, 0.0).astype(F32)
    scale = jnp.ones((R, 1), F32)
    for k in range(R):
        pivot = lax.rsqrt(state[k : k + 1, k : k + 1])
        row = state[k : k + 1, :] * pivot
        column = state[:, k : k + 1] * pivot
        below = state - column * row
        state = jnp.where(rows > k, below, jnp.where(rows == k, row, state))
        scale = jnp.where(rows[:, :1] == k, pivot, scale)
    return state[:, R : 2 * R], scale


def head_kernel(t_ref, out_ref):
    columns = out_ref.shape[1]
    inverse, scale = inverse_factor(t_ref[:, columns:])
    out_ref[...] = jnp.dot(
        inverse * scale, t_ref[:, :columns], precision=HIGHEST, preferred_element_type=F32
    )


def last_kernel(t_ref, s_ref, next_ref, basis_ref, coefficients_ref, summed_ref, *, rows_total):
    columns = t_ref.shape[1] - LANES
    inverse, _ = inverse_factor(t_ref[:, columns:])
    basis_ref[...] = (
        jnp.dot(inverse, s_ref[...], precision=HIGHEST, preferred_element_type=F32)
        * math.sqrt(rows_total)
    )
    coefficients = jnp.dot(
        inverse, t_ref[:, :columns], precision=HIGHEST, preferred_element_type=F32
    ) / math.sqrt(rows_total)
    width = N2 * N3
    modes = columns // width
    gram = jnp.zeros((R, R), F32)
    summed = jnp.zeros((R, width), F32)
    pieces = []
    for mode in range(modes):
        part = coefficients[:, mode * width : (mode + 1) * width]
        piece = lax.dot_general(
            next_ref[...], part, (((0,), (1,)), ((), ())), precision=HIGHEST,
            preferred_element_type=F32,
        )
        gram += lax.dot_general(piece, piece, NT, precision=HIGHEST, preferred_element_type=F32)
        summed += jnp.dot(piece, part, precision=HIGHEST, preferred_element_type=F32)
        pieces.append(piece)
    coefficients_ref[...] = jnp.concatenate(pieces, axis=1)
    gram = jnp.concatenate([gram, jnp.zeros((R, LANES - R), F32)], axis=1)
    summed_ref[...] = jnp.concatenate([summed, gram], axis=1)


def second_kernel(summed_ref, pieces_ref, frame_ref, remainder_ref, *, next_rows):
    width = N2 * N3
    inverse, _ = inverse_factor(summed_ref[:, width:])
    frame_ref[...] = jnp.dot(
        inverse, pieces_ref[...], precision=HIGHEST, preferred_element_type=F32
    ) * math.sqrt(next_rows)
    remainder_ref[...] = jnp.dot(
        inverse, summed_ref[:, :width], precision=HIGHEST, preferred_element_type=F32
    ) / math.sqrt(next_rows)


PARAMS = pltpu.CompilerParams(vmem_limit_bytes=32 * 1024 * 1024)


def times_rows(frame, a, block=512):
    rows, columns = a.shape
    return pl.pallas_call(
        rows_kernel,
        grid=(rows // block,),
        in_specs=[
            pl.BlockSpec((R, columns), lambda i: (0, 0)),
            pl.BlockSpec((block, columns), lambda i: (i, 0)),
        ],
        out_specs=pl.BlockSpec((R, block), lambda i: (0, i)),
        out_shape=jax.ShapeDtypeStruct((R, rows), F32),
        compiler_params=PARAMS,
        name="times_rows",
    )(frame, a)


def times_columns(s, a, block=512):
    rows, columns = a.shape
    return pl.pallas_call(
        columns_kernel,
        grid=(rows // block,),
        in_specs=[
            pl.BlockSpec((R, block), lambda i: (0, i)),
            pl.BlockSpec((block, columns), lambda i: (i, 0)),
        ],
        out_specs=pl.BlockSpec((R, columns + LANES), lambda i: (0, 0)),
        out_shape=jax.ShapeDtypeStruct((R, columns + LANES), F32),
        compiler_params=PARAMS,
        name="times_columns",
    )(s, a)


def swap(value, axis, bit):
    size = lax.axis_size(axis)
    return lax.ppermute(value, axis, [(i, i ^ bit) for i in range(size)])


def sum_doubling(value, axis):
    bit = 1
    while bit < lax.axis_size(axis):
        value = value + swap(value, axis, bit)
        bit *= 2
    return value


def sum_halved(value, axis):
    mine = lax.axis_index(axis) % 2
    half = value.shape[1] // 2
    low, high = value[:, :half], value[:, half:]
    kept = jnp.where(mine == 0, low, high) + swap(jnp.where(mine == 0, high, low), axis, 1)
    bit = 2
    while bit < lax.axis_size(axis):
        kept = kept + swap(kept, axis, bit)
        bit *= 2
    other = swap(kept, axis, 1)
    return jnp.concatenate(
        [jnp.where(mine == 0, kept, other), jnp.where(mine == 0, other, kept)], axis=1
    )


def shards(snapshots, sketch, sketch_next):
    rows, columns = snapshots.shape
    rows_total = rows * lax.axis_size("space")
    frame = sketch.T
    for step in range(ITERS + 1):
        s = sum_halved(times_rows(frame, snapshots), "param")
        t = sum_doubling(times_columns(s, snapshots), "space")
        if step < ITERS:
            frame = pl.pallas_call(
                head_kernel,
                out_shape=jax.ShapeDtypeStruct((R, columns), F32),
                compiler_params=PARAMS,
                name="head",
            )(t)
    width = N2 * N3
    local_next = columns // width * R
    basis, pieces, summed = pl.pallas_call(
        lambda *refs: last_kernel(*refs, rows_total=rows_total),
        out_shape=(
            jax.ShapeDtypeStruct((R, rows), F32),
            jax.ShapeDtypeStruct((R, local_next), F32),
            jax.ShapeDtypeStruct((R, width + LANES), F32),
        ),
        compiler_params=PARAMS,
        name="last",
    )(t, s, sketch_next)
    summed = sum_doubling(summed, "param")
    next_rows = local_next * lax.axis_size("param")
    second, remainder = pl.pallas_call(
        lambda *refs: second_kernel(*refs, next_rows=next_rows),
        out_shape=(
            jax.ShapeDtypeStruct((R, local_next), F32),
            jax.ShapeDtypeStruct((R, width), F32),
        ),
        compiler_params=PARAMS,
        name="second",
    )(summed, pieces)
    return basis, second, remainder


def solution(mesh):
    placed = (P("space", "param"), P("param", None), P())
    return jax.shard_map(
        shards,
        mesh=mesh,
        in_specs=placed,
        out_specs=(P(None, "space"), P(None, "param"), P()),
        check_vma=False,
    )
```

time: 888 us -> 284 us (0.32)
  waiting for transfers between devices: 405 us -> 112 us
  matrix products: 204 us -> 0 us
  blocking collectives: 200 us -> 0 us
  Pallas kernels: 0 us -> 137 us
  other arithmetic: 55 us -> 1.37 us
  starting transfers between devices: 0.33 us -> 30.4 us
  between operations: 14.8 us -> 0.96 us
    psum x8 -> x0, waiting for transfers between devices: 404 us -> none  [the longest x4 264 us: project(): return lax.psum(jnp.dot(basis, snapshots, precision=highest), 'space')]
    psum x9 -> x0, blocking collectives: 200 us -> none  [the longest x4 148 us: frame_space(): lower = jnp.linalg.cholesky(lax.psum(gram_matrix(block), 'space'))]
    dot_general x18 -> x0, matrix products: 191 us -> none  [the longest x3 79 us: shards(): lax.dot_general(column_frame, snapshots, (((1,), (1,)), ((), ())), precis...]
    pallas_call x0 -> x13, Pallas kernels: none -> 137 us  [the longest x4 62.3 us: times_rows(): pl.pallas_call(rows_kernel, grid=(rows // block,), in_specs=[pl.BlockSpec...]
    ppermute x0 -> x26, waiting for transfers between devices: none -> 112 us  [swap(): return lax.ppermute(value, axis, [(i, i ^ bit) for i in range(size)])]
    another operation x40 -> x0, other arithmetic: 53.4 us -> none  [the longest x16 24.7 us: apply_factor(): return jax.scipy.linalg.solve_triangular(lower, block, lower=True)]
    ppermute x0 -> x26, starting transfers between devices: none -> 30.4 us  [swap(): return lax.ppermute(value, axis, [(i, i ^ bit) for i in range(size)])]
    another operation x8 -> x0, matrix products: 13.4 us -> none  [apply_factor(): return jax.scipy.linalg.solve_triangular(lower, block, lower=True)]
  transfers between devices with their start and end apart: 8 -> 26, of which waited for: 8 -> 26; matrix products, arithmetic and copies ran while one was open for 0% -> 0% of each run, Pallas kernels for 0% -> 0%
where the time goes in v1:
time: 284 us; the launch traced here: 283 us
  Pallas kernels  137 us (48%)
  waiting for transfers between devices  112 us (39%)
  starting transfers between devices  30.4 us (11%)
    ppermute x26, waiting for transfers between devices, swap(): return lax.ppermute(value, axis, [(i, i ^ bit) for i in range(size)])  112 us
    pallas_call x4, Pallas kernels, times_rows(): pl.pallas_call(rows_kernel, grid=(rows // block,), in_specs=[pl.BlockSpec...  62.3 us
    pallas_call x4, Pallas kernels, times_columns(): pl.pallas_call(columns_kernel, grid=(rows // block,), in_specs=[pl.BlockS...  57.4 us
    ppermute x26, starting transfers between devices, swap(): return lax.ppermute(value, axis, [(i, i ^ bit) for i in range(size)])  30.4 us
    pallas_call x3, Pallas kernels, shards(): pl.pallas_call(head_kernel, out_shape=jax.ShapeDtypeStruct((R, columns),...  9.12 us
  transfers between devices with their start and end apart: 26, of which 26 were waited for; matrix products, arithmetic and copies ran while one was open for 0% of the time, Pallas kernels for 0%

profile of v1, /device:TPU:0, one launch (start us, length us, event | category | flops | bytes accessed | tf_op | source)
XLA Modules:
  0.0 282.7 jit_solution(12564811290738776849)
XLA Ops:
  1.5 15.6 %times_rows.4 = f32[32,6144]{1,0:T(8,128)S(1)} custom-call(f32[32,1024]{1,0:T(8,128)S(1)} %bitcast.1, f32[6144,1024]{1,0:T(8,128)} %a_ref.15), custom_call_target="tpu_custom_call" | custom-call | tf_op jit(solution)/shard_map/times_rows/pallas_call | solution.py:124
  19.1 2.9 %collective-permute-start.1 = (f32[32,3072]{1,0:T(8,128)S(1)}, f32[32,3072]{1,0:T(8,128)S(1)}, u32[]{:S(2)}, u32[]{:S(2)}) collective-permute-start(f32[32,3072]{1,0:T(8,128)S(1)} %select_add_fusion.3), channel_id=1, source_target_pairs={{0,2},{1,3},{2,0},{3,1},{4,6},{5,7},{6,4},{7,5},{8,10},{9,11},{10,... | collective-permute-start | bytes 1179656 | tf_op jit(solution)/shard_map/ppermute | solution.py:156
  22.1 9.4 %collective-permute-done.1 = f32[32,3072]{1,0:T(8,128)S(1)} collective-permute-done((f32[32,3072]{1,0:T(8,128)S(1)}, f32[32,3072]{1,0:T(8,128)S(1)}, u32[]{:S(2)}, u32[]{:S(2)}) %collective-permute-start.1) | collective-permute-done | bytes 393248 | tf_op jit(solution)/shard_map/ppermute | solution.py:156
  31.6 1.7 collective-permute-done.2
  33.4 14.3 %times_columns.4 = f32[32,1152]{1,0:T(8,128)S(1)} custom-call(f32[32,6144]{1,0:T(8,128)S(1)} %pad_maximum_fusion.s_ref, f32[6144,1024]{1,0:T(8,128)} %a_ref.15), custom_call_target="tpu_custom_call" | custom-call | tf_op jit(solution)/shard_map/times_columns/pallas_call | solution.py:140
  47.8 1.8 collective-permute-start.3
  49.6 4.2 %collective-permute-done.3 = f32[32,1152]{1,0:T(8,128)S(1)} collective-permute-done((f32[32,1152]{1,0:T(8,128)S(1)}, f32[32,1152]{1,0:T(8,128)S(1)}, u32[]{:S(2)}, u32[]{:S(2)}) %collective-permute-start.3) | collective-permute-done | bytes 147488 | tf_op jit(solution)/shard_map/ppermute | solution.py:156
  53.8 1.9 collective-permute-start.4
  55.6 3.4 %collective-permute-done.4 = f32[32,1152]{1,0:T(8,128)S(1)} collective-permute-done((f32[32,1152]{1,0:T(8,128)S(1)}, f32[32,1152]{1,0:T(8,128)S(1)}, u32[]{:S(2)}, u32[]{:S(2)}) %collective-permute-start.4) | collective-permute-done | bytes 147488 | tf_op jit(solution)/shard_map/ppermute | solution.py:156
  59.0 2.9 %collective-permute-start.5 = (f32[32,1152]{1,0:T(8,128)S(1)}, f32[32,1152]{1,0:T(8,128)S(1)}, u32[]{:S(2)}, u32[]{:S(2)}) collective-permute-start(f32[32,1152]{1,0:T(8,128)S(1)} %add.77), channel_id=1, source_target_pairs={{0,16},{4,20},{8,24},{12,28},{16,0},{20,4},{24,8},{28,12},{1,17},{... | collective-permute-start | bytes 442376 | tf_op jit(solution)/shard_map/ppermute | solution.py:156
  61.9 5.3 %collective-permute-done.5 = f32[32,1152]{1,0:T(8,128)S(1)} collective-permute-done((f32[32,1152]{1,0:T(8,128)S(1)}, f32[32,1152]{1,0:T(8,128)S(1)}, u32[]{:S(2)}, u32[]{:S(2)}) %collective-permute-start.5) | collective-permute-done | bytes 147488 | tf_op jit(solution)/shard_map/ppermute | solution.py:156
  67.2 3.0 %head.3.frame_ref = f32[32,1024]{1,0:T(8,128)S(1)} custom-call(f32[32,1152]{1,0:T(8,128)S(1)} %add.78.t_ref), custom_call_target="tpu_custom_call" | custom-call | tf_op jit(solution)/shard_map/head/pallas_call | solution.py:190
  70.3 15.6 %times_rows.5 = f32[32,6144]{1,0:T(8,128)S(1)} custom-call(f32[32,1024]{1,0:T(8,128)S(1)} %head.3.frame_ref, f32[6144,1024]{1,0:T(8,128)} %a_ref.15), custom_call_target="tpu_custom_call" | custom-call | tf_op jit(solution)/shard_map/times_rows/pallas_call | solution.py:124
  86.0 1.7 collective-permute-done.6
  87.8 1.6 collective-permute-start.7
  89.4 9.6 %collective-permute-done.7 = f32[32,3072]{1,0:T(8,128)S(1)} collective-permute-done((f32[32,3072]{1,0:T(8,128)S(1)}, f32[32,3072]{1,0:T(8,128)S(1)}, u32[]{:S(2)}, u32[]{:S(2)}) %collective-permute-start.7) | collective-permute-done | bytes 393248 | tf_op jit(solution)/shard_map/ppermute | solution.py:156
  99.1 1.7 collective-permute-done.8
  101.0 14.3 %times_columns.5 = f32[32,1152]{1,0:T(8,128)S(1)} custom-call(f32[32,6144]{1,0:T(8,128)S(1)} %pad_maximum_fusion.1.s_ref, f32[6144,1024]{1,0:T(8,128)} %a_ref.15), custom_call_target="tpu_custom_call" | custom-call | tf_op jit(solution)/shard_map/times_columns/pallas_call | solution.py:140
  115.3 1.6 collective-permute-start.9
  117.0 4.3 %collective-permute-done.9 = f32[32,1152]{1,0:T(8,128)S(1)} collective-permute-done((f32[32,1152]{1,0:T(8,128)S(1)}, f32[32,1152]{1,0:T(8,128)S(1)}, u32[]{:S(2)}, u32[]{:S(2)}) %collective-permute-start.9) | collective-permute-done | bytes 147488 | tf_op jit(solution)/shard_map/ppermute | solution.py:156
  122.1 4.4 %collective-permute-done.10 = f32[32,1152]{1,0:T(8,128)S(1)} collective-permute-done((f32[32,1152]{1,0:T(8,128)S(1)}, f32[32,1152]{1,0:T(8,128)S(1)}, u32[]{:S(2)}, u32[]{:S(2)}) %collective-permute-start.10) | collective-permute-done | bytes 147488 | tf_op jit(solution)/shard_map/ppermute | solution.py:156
  126.5 2.3 collective-permute-start.11
  128.9 5.9 %collective-permute-done.11 = f32[32,1152]{1,0:T(8,128)S(1)} collective-permute-done((f32[32,1152]{1,0:T(8,128)S(1)}, f32[32,1152]{1,0:T(8,128)S(1)}, u32[]{:S(2)}, u32[]{:S(2)}) %collective-permute-start.11) | collective-permute-done | bytes 147488 | tf_op jit(solution)/shard_map/ppermute | solution.py:156
  134.7 3.0 %head.4.frame_ref = f32[32,1024]{1,0:T(8,128)S(1)} custom-call(f32[32,1152]{1,0:T(8,128)S(1)} %add.83.t_ref), custom_call_target="tpu_custom_call" | custom-call | tf_op jit(solution)/shard_map/head/pallas_call | solution.py:190
  137.8 15.6 %times_rows.6 = f32[32,6144]{1,0:T(8,128)S(1)} custom-call(f32[32,1024]{1,0:T(8,128)S(1)} %head.4.frame_ref, f32[6144,1024]{1,0:T(8,128)} %a_ref.15), custom_call_target="tpu_custom_call" | custom-call | tf_op jit(solution)/shard_map/times_rows/pallas_call | solution.py:124
  153.5 1.7 collective-permute-done.12
  156.9 9.7 %collective-permute-done.13 = f32[32,3072]{1,0:T(8,128)S(1)} collective-permute-done((f32[32,3072]{1,0:T(8,128)S(1)}, f32[32,3072]{1,0:T(8,128)S(1)}, u32[]{:S(2)}, u32[]{:S(2)}) %collective-permute-start.13) | collective-permute-done | bytes 393248 | tf_op jit(solution)/shard_map/ppermute | solution.py:156
  166.6 1.7 collective-permute-done.14
  168.5 14.3 %times_columns.6 = f32[32,1152]{1,0:T(8,128)S(1)} custom-call(f32[32,6144]{1,0:T(8,128)S(1)} %pad_maximum_fusion.2.s_ref, f32[6144,1024]{1,0:T(8,128)} %a_ref.15), custom_call_target="tpu_custom_call" | custom-call | tf_op jit(solution)/shard_map/times_columns/pallas_call | solution.py:140
  182.8 1.6 collective-permute-start.15
  184.4 4.4 %collective-permute-done.15 = f32[32,1152]{1,0:T(8,128)S(1)} collective-permute-done((f32[32,1152]{1,0:T(8,128)S(1)}, f32[32,1152]{1,0:T(8,128)S(1)}, u32[]{:S(2)}, u32[]{:S(2)}) %collective-permute-start.15) | collective-permute-done | bytes 147488 | tf_op jit(solution)/shard_map/ppermute | solution.py:156
  189.4 4.6 %collective-permute-done.16 = f32[32,1152]{1,0:T(8,128)S(1)} collective-permute-done((f32[32,1152]{1,0:T(8,128)S(1)}, f32[32,1152]{1,0:T(8,128)S(1)}, u32[]{:S(2)}, u32[]{:S(2)}) %collective-permute-start.16) | collective-permute-done | bytes 147488 | tf_op jit(solution)/shard_map/ppermute | solution.py:156
  194.0 2.2 collective-permute-start.17
  196.2 5.9 %collective-permute-done.17 = f32[32,1152]{1,0:T(8,128)S(1)} collective-permute-done((f32[32,1152]{1,0:T(8,128)S(1)}, f32[32,1152]{1,0:T(8,128)S(1)}, u32[]{:S(2)}, u32[]{:S(2)}) %collective-permute-start.17) | collective-permute-done | bytes 147488 | tf_op jit(solution)/shard_map/ppermute | solution.py:156
  202.1 3.0 %head.5.frame_ref = f32[32,1024]{1,0:T(8,128)S(1)} custom-call(f32[32,1152]{1,0:T(8,128)S(1)} %add.88.t_ref), custom_call_target="tpu_custom_call" | custom-call | tf_op jit(solution)/shard_map/head/pallas_call | solution.py:190
  205.1 15.6 %times_rows.7 = f32[32,6144]{1,0:T(8,128)S(1)} custom-call(f32[32,1024]{1,0:T(8,128)S(1)} %head.5.frame_ref, f32[6144,1024]{1,0:T(8,128)} %a_ref.15), custom_call_target="tpu_custom_call" | custom-call | tf_op jit(solution)/shard_map/times_rows/pallas_call | solution.py:124
  220.8 1.7 collective-permute-done.18
  224.2 9.7 %collective-permute-done.19 = f32[32,3072]{1,0:T(8,128)S(1)} collective-permute-done((f32[32,3072]{1,0:T(8,128)S(1)}, f32[32,3072]{1,0:T(8,128)S(1)}, u32[]{:S(2)}, u32[]{:S(2)}) %collective-permute-start.19) | collective-permute-done | bytes 393248 | tf_op jit(solution)/shard_map/ppermute | solution.py:156
  234.0 1.7 collective-permute-done.20
  235.8 14.3 %times_columns.7 = f32[32,1152]{1,0:T(8,128)S(1)} custom-call(f32[32,6144]{1,0:T(8,128)S(1)} %pad_maximum_fusion.3.s_ref.refs_1_, f32[6144,1024]{1,0:T(8,128)} %a_ref.15), custom_call_target="tpu_custom_call" | custom-call | tf_op jit(solution)/shard_map/times_columns/pallas_call | solution.py:140
  250.2 1.6 collective-permute-start.21
  251.8 4.4 %collective-permute-done.21 = f32[32,1152]{1,0:T(8,128)S(1)} collective-permute-done((f32[32,1152]{1,0:T(8,128)S(1)}, f32[32,1152]{1,0:T(8,128)S(1)}, u32[]{:S(2)}, u32[]{:S(2)}) %collective-permute-start.21) | collective-permute-done | bytes 147488 | tf_op jit(solution)/shard_map/ppermute | solution.py:156
  256.8 4.6 %collective-permute-done.22 = f32[32,1152]{1,0:T(8,128)S(1)} collective-permute-done((f32[32,1152]{1,0:T(8,128)S(1)}, f32[32,1152]{1,0:T(8,128)S(1)}, u32[]{:S(2)}, u32[]{:S(2)}) %collective-permute-start.22) | collective-permute-done | bytes 147488 | tf_op jit(solution)/shard_map/ppermute | solution.py:156
  261.4 2.2 collective-permute-start.23
  263.7 5.8 %collective-permute-done.23 = f32[32,1152]{1,0:T(8,128)S(1)} collective-permute-done((f32[32,1152]{1,0:T(8,128)S(1)}, f32[32,1152]{1,0:T(8,128)S(1)}, u32[]{:S(2)}, u32[]{:S(2)}) %collective-permute-start.23) | collective-permute-done | bytes 147488 | tf_op jit(solution)/shard_map/ppermute | solution.py:156
  269.4 4.3 %last.1 = (f32[32,6144]{1,0:T(8,128)}, f32[32,128]{1,0:T(8,128)S(1)}, f32[32,384]{1,0:T(8,128)S(1)}) custom-call(f32[32,1152]{1,0:T(8,128)S(1)} %add.93.refs_0_, f32[32,6144]{1,0:T(8,128)S(1)} %pad_maximum_fusion.3.s_ref.refs_1_, f32[256,32]{1,0:T(8,128)S(1)} %copy.6.refs_2_), custom_call_target="tpu_custom_call" | custom-call | tf_op jit(solution)/shard_map/last/pallas_call | solution.py:198
  276.7 2.6 collective-permute-done.25
  279.3 3.5 %second.1 = (f32[32,128]{1,0:T(8,128)}, f32[32,256]{1,0:T(8,128)}) custom-call(f32[32,384]{1,0:T(8,128)S(1)} %add.95.refs_0_, f32[32,128]{1,0:T(8,128)S(1)} %get-tuple-element.10.refs_1_), custom_call_target="tpu_custom_call" | custom-call | tf_op jit(solution)/shard_map/second/pallas_call | solution.py:210
  (56 shorter events, 12.8 us)
Async XLA Ops:
  0.6 0.9 copy-start
  17.2 1.9 collective-permute-start
  19.1 12.3 %collective-permute-start.1 = (f32[32,3072]{1,0:T(8,128)S(1)}, f32[32,3072]{1,0:T(8,128)S(1)}, u32[]{:S(2)}, u32[]{:S(2)}) collective-permute-start(f32[32,3072]{1,0:T(8,128)S(1)} %select_add_fusion.3), channel_id=1, source_target_pairs={{0,2},{1,3},{2,0},{3,1},{4,6},{5,7},{6,4},{7,5},{8,10},{9,11},{10,... | collective-permute-start | bytes 1179656 | tf_op jit(solution)/shard_map/ppermute | solution.py:156
  31.5 1.8 collective-permute-start.2
  47.8 6.0 %collective-permute-start.3 = (f32[32,1152]{1,0:T(8,128)S(1)}, f32[32,1152]{1,0:T(8,128)S(1)}, u32[]{:S(2)}, u32[]{:S(2)}) collective-permute-start(f32[32,1152]{1,0:T(8,128)S(1)} %times_columns.4), channel_id=1, source_target_pairs={{0,4},{4,0},{8,12},{12,8},{16,20},{20,16},{24,28},{28,24},{1,5},{5... | collective-permute-start | bytes 442376 | tf_op jit(solution)/shard_map/ppermute | solution.py:156
  53.8 5.2 %collective-permute-start.4 = (f32[32,1152]{1,0:T(8,128)S(1)}, f32[32,1152]{1,0:T(8,128)S(1)}, u32[]{:S(2)}, u32[]{:S(2)}) collective-permute-start(f32[32,1152]{1,0:T(8,128)S(1)} %add.76), channel_id=1, source_target_pairs={{0,8},{4,12},{8,0},{12,4},{16,24},{20,28},{24,16},{28,20},{1,9},{5... | collective-permute-start | bytes 442376 | tf_op jit(solution)/shard_map/ppermute | solution.py:156
  59.0 8.2 %collective-permute-start.5 = (f32[32,1152]{1,0:T(8,128)S(1)}, f32[32,1152]{1,0:T(8,128)S(1)}, u32[]{:S(2)}, u32[]{:S(2)}) collective-permute-start(f32[32,1152]{1,0:T(8,128)S(1)} %add.77), channel_id=1, source_target_pairs={{0,16},{4,20},{8,24},{12,28},{16,0},{20,4},{24,8},{28,12},{1,17},{... | collective-permute-start | bytes 442376 | tf_op jit(solution)/shard_map/ppermute | solution.py:156
  85.9 1.8 collective-permute-start.6
  87.8 11.2 %collective-permute-start.7 = (f32[32,3072]{1,0:T(8,128)S(1)}, f32[32,3072]{1,0:T(8,128)S(1)}, u32[]{:S(2)}, u32[]{:S(2)}) collective-permute-start(f32[32,3072]{1,0:T(8,128)S(1)} %select_add_fusion.2), channel_id=1, source_target_pairs={{0,2},{1,3},{2,0},{3,1},{4,6},{5,7},{6,4},{7,5},{8,10},{9,11},{10,... | collective-permute-start | bytes 1179656 | tf_op jit(solution)/shard_map/ppermute | solution.py:156
  99.1 1.8 collective-permute-start.8
  115.3 6.0 %collective-permute-start.9 = (f32[32,1152]{1,0:T(8,128)S(1)}, f32[32,1152]{1,0:T(8,128)S(1)}, u32[]{:S(2)}, u32[]{:S(2)}) collective-permute-start(f32[32,1152]{1,0:T(8,128)S(1)} %times_columns.5), channel_id=1, source_target_pairs={{0,4},{4,0},{8,12},{12,8},{16,20},{20,16},{24,28},{28,24},{1,5},{5... | collective-permute-start | bytes 442376 | tf_op jit(solution)/shard_map/ppermute | solution.py:156
  121.3 5.2 %collective-permute-start.10 = (f32[32,1152]{1,0:T(8,128)S(1)}, f32[32,1152]{1,0:T(8,128)S(1)}, u32[]{:S(2)}, u32[]{:S(2)}) collective-permute-start(f32[32,1152]{1,0:T(8,128)S(1)} %add.81), channel_id=1, source_target_pairs={{0,8},{4,12},{8,0},{12,4},{16,24},{20,28},{24,16},{28,20},{1,9},{5... | collective-permute-start | bytes 442376 | tf_op jit(solution)/shard_map/ppermute | solution.py:156
  126.5 8.2 %collective-permute-start.11 = (f32[32,1152]{1,0:T(8,128)S(1)}, f32[32,1152]{1,0:T(8,128)S(1)}, u32[]{:S(2)}, u32[]{:S(2)}) collective-permute-start(f32[32,1152]{1,0:T(8,128)S(1)} %add.82), channel_id=1, source_target_pairs={{0,16},{4,20},{8,24},{12,28},{16,0},{20,4},{24,8},{28,12},{1,17},{... | collective-permute-start | bytes 442376 | tf_op jit(solution)/shard_map/ppermute | solution.py:156
  153.4 1.8 collective-permute-start.12
  155.3 11.2 %collective-permute-start.13 = (f32[32,3072]{1,0:T(8,128)S(1)}, f32[32,3072]{1,0:T(8,128)S(1)}, u32[]{:S(2)}, u32[]{:S(2)}) collective-permute-start(f32[32,3072]{1,0:T(8,128)S(1)} %select_add_fusion.1), channel_id=1, source_target_pairs={{0,2},{1,3},{2,0},{3,1},{4,6},{5,7},{6,4},{7,5},{8,10},{9,11},{10,... | collective-permute-start | bytes 1179656 | tf_op jit(solution)/shard_map/ppermute | solution.py:156
  166.6 1.8 collective-permute-start.14
  182.8 6.0 %collective-permute-start.15 = (f32[32,1152]{1,0:T(8,128)S(1)}, f32[32,1152]{1,0:T(8,128)S(1)}, u32[]{:S(2)}, u32[]{:S(2)}) collective-permute-start(f32[32,1152]{1,0:T(8,128)S(1)} %times_columns.6), channel_id=1, source_target_pairs={{0,4},{4,0},{8,12},{12,8},{16,20},{20,16},{24,28},{28,24},{1,5},{5... | collective-permute-start | bytes 442376 | tf_op jit(solution)/shard_map/ppermute | solution.py:156
  188.8 5.2 %collective-permute-start.16 = (f32[32,1152]{1,0:T(8,128)S(1)}, f32[32,1152]{1,0:T(8,128)S(1)}, u32[]{:S(2)}, u32[]{:S(2)}) collective-permute-start(f32[32,1152]{1,0:T(8,128)S(1)} %add.86), channel_id=1, source_target_pairs={{0,8},{4,12},{8,0},{12,4},{16,24},{20,28},{24,16},{28,20},{1,9},{5... | collective-permute-start | bytes 442376 | tf_op jit(solution)/shard_map/ppermute | solution.py:156
  194.0 8.0 %collective-permute-start.17 = (f32[32,1152]{1,0:T(8,128)S(1)}, f32[32,1152]{1,0:T(8,128)S(1)}, u32[]{:S(2)}, u32[]{:S(2)}) collective-permute-start(f32[32,1152]{1,0:T(8,128)S(1)} %add.87), channel_id=1, source_target_pairs={{0,16},{4,20},{8,24},{12,28},{16,0},{20,4},{24,8},{28,12},{1,17},{... | collective-permute-start | bytes 442376 | tf_op jit(solution)/shard_map/ppermute | solution.py:156
  205.1 58.5 %copy-start.1 = (f32[256,32]{0,1:T(8,128)S(1)}, f32[256,32]{0,1:T(8,128)}, u32[]{:S(2)}) copy-start(f32[256,32]{0,1:T(8,128)} %param.5) | copy-start | bytes 98308
  220.8 1.8 collective-permute-start.18
  222.6 11.2 %collective-permute-start.19 = (f32[32,3072]{1,0:T(8,128)S(1)}, f32[32,3072]{1,0:T(8,128)S(1)}, u32[]{:S(2)}, u32[]{:S(2)}) collective-permute-start(f32[32,3072]{1,0:T(8,128)S(1)} %select_add_fusion), channel_id=1, source_target_pairs={{0,2},{1,3},{2,0},{3,1},{4,6},{5,7},{6,4},{7,5},{8,10},{9,11},{10,... | collective-permute-start | bytes 1179656 | tf_op jit(solution)/shard_map/ppermute | solution.py:156
  233.9 1.8 collective-permute-start.20
  250.2 6.0 %collective-permute-start.21 = (f32[32,1152]{1,0:T(8,128)S(1)}, f32[32,1152]{1,0:T(8,128)S(1)}, u32[]{:S(2)}, u32[]{:S(2)}) collective-permute-start(f32[32,1152]{1,0:T(8,128)S(1)} %times_columns.7), channel_id=1, source_target_pairs={{0,4},{4,0},{8,12},{12,8},{16,20},{20,16},{24,28},{28,24},{1,5},{5... | collective-permute-start | bytes 442376 | tf_op jit(solution)/shard_map/ppermute | solution.py:156
  256.2 5.2 %collective-permute-start.22 = (f32[32,1152]{1,0:T(8,128)S(1)}, f32[32,1152]{1,0:T(8,128)S(1)}, u32[]{:S(2)}, u32[]{:S(2)}) collective-permute-start(f32[32,1152]{1,0:T(8,128)S(1)} %add.91), channel_id=1, source_target_pairs={{0,8},{4,12},{8,0},{12,4},{16,24},{20,28},{24,16},{28,20},{1,9},{5... | collective-permute-start | bytes 442376 | tf_op jit(solution)/shard_map/ppermute | solution.py:156
  261.4 8.0 %collective-permute-start.23 = (f32[32,1152]{1,0:T(8,128)S(1)}, f32[32,1152]{1,0:T(8,128)S(1)}, u32[]{:S(2)}, u32[]{:S(2)}) collective-permute-start(f32[32,1152]{1,0:T(8,128)S(1)} %add.92), channel_id=1, source_target_pairs={{0,16},{4,20},{8,24},{12,28},{16,0},{20,4},{24,8},{28,12},{1,17},{... | collective-permute-start | bytes 442376 | tf_op jit(solution)/shard_map/ppermute | solution.py:156
  273.8 1.3 collective-permute-start.24
  275.1 4.2 %collective-permute-start.25 = (f32[32,384]{1,0:T(8,128)S(1)}, f32[32,384]{1,0:T(8,128)S(1)}, u32[]{:S(2)}, u32[]{:S(2)}) collective-permute-start(f32[32,384]{1,0:T(8,128)S(1)} %add.94), channel_id=1, source_target_pairs={{0,2},{1,3},{2,0},{3,1},{4,6},{5,7},{6,4},{7,5},{8,10},{9,11},{10,... | collective-permute-start | bytes 147464 | tf_op jit(solution)/shard_map/ppermute | solution.py:156

commit v2 on v1

--- a/solution.py
+++ b/solution.py
@@ -23,34 +23,68 @@
     return high, (block - high.astype(F32)).astype(BF16)
 
 
-def rows_kernel(frame_ref, a_ref, out_ref):
-    frame_high, frame_low = split(frame_ref[...])
-    both = jnp.concatenate([frame_high, frame_low], axis=0)
-    high, low = split(a_ref[...])
-    first = lax.dot_general(both, high, NT, preferred_element_type=F32)
-    second = lax.dot_general(frame_high, low, NT, preferred_element_type=F32)
-    out_ref[...] = first[:R] + (first[R:] + second)
-
-
-def columns_kernel(s_ref, a_ref, out_ref):
-    s = s_ref[...]
-    s_high, s_low = split(s)
-    both = jnp.concatenate([s_high, s_low], axis=0)
-    high, low = split(a_ref[...])
-    first = jnp.dot(both, high, preferred_element_type=F32)
-    second = jnp.dot(s_high, low, preferred_element_type=F32)
-    product = first[:R] + (first[R:] + second)
-    gram = lax.dot_general(s, s, NT, precision=HIGHEST, preferred_element_type=F32)
-    gram = jnp.concatenate([gram, jnp.zeros((R, LANES - R), F32)], axis=1)
-    whole = jnp.concatenate([product, gram], axis=1)
-
-    @pl.when(pl.program_id(0) == 0)
-    def _():
-        out_ref[...] = whole
-
-    @pl.when(pl.program_id(0) > 0)
-    def _():
-        out_ref[...] += whole
+def stacked(block):
+    return jnp.concatenate(split(block), axis=0)
+
+
+def folded(product):
+    turned = product.T
+    return turned[:R] + turned[R:]
+
+
+def rows_kernel(frame_ref, a_ref, out_ref, tall_ref=None):
+    block, columns = a_ref.shape
+    a = a_ref[...]
+    high, low = split(a)
+    frame = stacked(frame_ref[...])
+    product = lax.dot_general(high, frame, NT, preferred_element_type=F32)
+    product += lax.dot_general(low, frame, NT, preferred_element_type=F32)
+    out_ref[...] = folded(product)
+    if tall_ref is not None:
+        at = pl.ds(pl.multiple_of(pl.program_id(0) * block, block), block)
+        turned_high, turned_low = split(a.T)
+        tall_ref[:columns, at] = turned_high
+        tall_ref[columns:, at] = turned_low
+
+
+def columns_kernel(s_ref, tall_ref, out_ref, sum_ref, *, block):
+    columns = tall_ref.shape[0] // 2
+    sum_ref[...] = jnp.zeros_like(sum_ref)
+
+    def body(i, carry):
+        at = pl.ds(pl.multiple_of(i * block, block), block)
+        s = stacked(s_ref[:, at])
+        left = jnp.concatenate([tall_ref[:, at], s], axis=0)
+        sum_ref[...] += lax.dot_general(left, s, NT, preferred_element_type=F32)
+        return carry
+
+    lax.fori_loop(0, s_ref.shape[1] // block, body, 0)
+    product = folded(sum_ref[:columns] + sum_ref[columns : 2 * columns])
+    both = sum_ref[2 * columns :]
+    gram = both[:R] + both[R:]
+    gram = gram[:, :R] + gram[:, R:]
+    if out_ref.ndim == 2:
+        out_ref[:, :columns] = product
+        out_ref[:, columns:] = jnp.zeros((R, LANES), F32)
+        out_ref[:, columns : columns + R] = gram
+    else:
+        parts = out_ref.shape[0]
+        rows = R // parts
+        out_ref[...] = jnp.zeros_like(out_ref)
+        for j in range(parts):
+            out_ref[j, :R, :] = product[:, j * LANES : (j + 1) * LANES]
+            out_ref[j, R : R + rows, :R] = gram[j * rows : (j + 1) * rows]
+
+
+def unpacked(t_ref):
+    if len(t_ref.shape) == 2:
+        columns = t_ref.shape[1] - LANES
+        return t_ref[:, :columns], t_ref[:, columns:]
+    parts = t_ref.shape[0]
+    rows = R // parts
+    product = jnp.concatenate([t_ref[j, :R, :] for j in range(parts)], axis=1)
+    gram = jnp.concatenate([t_ref[j, R : R + rows, :] for j in range(parts)], axis=0)
+    return product, gram
 
 
 def inverse_factor(gram):
@@ -69,22 +103,23 @@
 
 
 def head_kernel(t_ref, out_ref):
-    columns = out_ref.shape[1]
-    inverse, scale = inverse_factor(t_ref[:, columns:])
+    product, gram = unpacked(t_ref)
+    inverse, scale = inverse_factor(gram)
     out_ref[...] = jnp.dot(
-        inverse * scale, t_ref[:, :columns], precision=HIGHEST, preferred_element_type=F32
+        inverse * scale, product, precision=HIGHEST, preferred_element_type=F32
     )
 
 
 def last_kernel(t_ref, s_ref, next_ref, basis_ref, coefficients_ref, summed_ref, *, rows_total):
-    columns = t_ref.shape[1] - LANES
-    inverse, _ = inverse_factor(t_ref[:, columns:])
+    product, gram = unpacked(t_ref)
+    columns = product.shape[1]
+    inverse, _ = inverse_factor(gram)
     basis_ref[...] = (
         jnp.dot(inverse, s_ref[...], precision=HIGHEST, preferred_element_type=F32)
         * math.sqrt(rows_total)
     )
     coefficients = jnp.dot(
-        inverse, t_ref[:, :columns], precision=HIGHEST, preferred_element_type=F32
+        inverse, product, precision=HIGHEST, preferred_element_type=F32
     ) / math.sqrt(rows_total)
     width = N2 * N3
     modes = columns // width
@@ -116,11 +151,18 @@
     ) / math.sqrt(next_rows)
 
 
-PARAMS = pltpu.CompilerParams(vmem_limit_bytes=32 * 1024 * 1024)
-
-
-def times_rows(frame, a, block=512):
+def params(mebibytes):
+    return pltpu.CompilerParams(vmem_limit_bytes=mebibytes * 1024 * 1024)
+
+
+WHOLE = pl.BlockSpec(memory_space=pltpu.VMEM)
+
+
+def times_rows(frame, a, keep=False, block=512):
     rows, columns = a.shape
+    a = pltpu.with_memory_space_constraint(a, pltpu.HBM)
+    out_spec = pl.BlockSpec((R, block), lambda i: (0, i))
+    out_shape = jax.ShapeDtypeStruct((R, rows), F32)
     return pl.pallas_call(
         rows_kernel,
         grid=(rows // block,),
@@ -128,27 +170,26 @@
             pl.BlockSpec((R, columns), lambda i: (0, 0)),
             pl.BlockSpec((block, columns), lambda i: (i, 0)),
         ],
-        out_specs=pl.BlockSpec((R, block), lambda i: (0, i)),
-        out_shape=jax.ShapeDtypeStruct((R, rows), F32),
-        compiler_params=PARAMS,
+        out_specs=(out_spec, WHOLE) if keep else out_spec,
+        out_shape=(out_shape, pltpu.VMEM((2 * columns, rows), BF16)) if keep else out_shape,
+        compiler_params=params(24),
         name="times_rows",
     )(frame, a)
 
 
-def times_columns(s, a, block=512):
-    rows, columns = a.shape
+def times_columns(s, tall, parts, block=1536):
+    columns = tall.shape[0] // 2
+    shape = (parts, R + 8, LANES) if parts * LANES == columns else (R, columns + LANES)
+    tall = pltpu.with_memory_space_constraint(tall, pltpu.VMEM)
     return pl.pallas_call(
-        columns_kernel,
-        grid=(rows // block,),
-        in_specs=[
-            pl.BlockSpec((R, block), lambda i: (0, i)),
-            pl.BlockSpec((block, columns), lambda i: (i, 0)),
-        ],
-        out_specs=pl.BlockSpec((R, columns + LANES), lambda i: (0, 0)),
-        out_shape=jax.ShapeDtypeStruct((R, columns + LANES), F32),
-        compiler_params=PARAMS,
+        lambda *refs: columns_kernel(*refs, block=block),
+        in_specs=[WHOLE, WHOLE],
+        out_specs=WHOLE,
+        out_shape=jax.ShapeDtypeStruct(shape, F32),
+        scratch_shapes=[pltpu.VMEM((2 * columns + 2 * R, 2 * R), F32)],
+        compiler_params=params(8),
         name="times_columns",
-    )(s, a)
+    )(s, tall)
 
 
 def swap(value, axis, bit):
@@ -179,18 +220,28 @@
     )
 
 
+def sum_parts(value, axis):
+    if value.ndim == 2:
+        return sum_doubling(value, axis)
+    mine = jnp.sum(lax.all_to_all(value, axis, 0, 0, tiled=True), axis=0, keepdims=True)
+    return lax.all_to_all(jnp.broadcast_to(mine, value.shape), axis, 0, 0, tiled=True)
+
+
 def shards(snapshots, sketch, sketch_next):
     rows, columns = snapshots.shape
     rows_total = rows * lax.axis_size("space")
     frame = sketch.T
+    s, tall = times_rows(frame, snapshots, keep=True)
     for step in range(ITERS + 1):
-        s = sum_halved(times_rows(frame, snapshots), "param")
-        t = sum_doubling(times_columns(s, snapshots), "space")
+        if step:
+            s = times_rows(frame, snapshots)
+        s = sum_halved(s, "param")
+        t = sum_parts(times_columns(s, tall, lax.axis_size("space")), "space")
         if step < ITERS:
             frame = pl.pallas_call(
                 head_kernel,
                 out_shape=jax.ShapeDtypeStruct((R, columns), F32),
-                compiler_params=PARAMS,
+                compiler_params=params(8),
                 name="head",
             )(t)
     width = N2 * N3
@@ -202,7 +253,7 @@
             jax.ShapeDtypeStruct((R, local_next), F32),
             jax.ShapeDtypeStruct((R, width + LANES), F32),
         ),
-        compiler_params=PARAMS,
+        compiler_params=params(8),
         name="last",
     )(t, s, sketch_next)
     summed = sum_doubling(summed, "param")
@@ -213,7 +264,7 @@
             jax.ShapeDtypeStruct((R, local_next), F32),
             jax.ShapeDtypeStruct((R, width), F32),
         ),
-        compiler_params=PARAMS,
+        compiler_params=params(8),
         name="second",
     )(summed, pieces)
     return basis, second, remainder

time: 284 us -> 294 us (1.035)
  blocking collectives: 0 us -> 76.3 us
  waiting for transfers between devices: 112 us -> 62.9 us
  Pallas kernels: 137 us -> 111 us
  local copies, waits for them, and re-layouts: 1 us -> 26.3 us
  starting transfers between devices: 30.4 us -> 13.6 us
    all_to_all x0 -> x7, blocking collectives: none -> 76.3 us  [the longest x4 45.2 us: sum_parts(): lax.all_to_all(value, axis, 0, 0, tiled=True)]
    ppermute x26 -> x14, waiting for transfers between devices: 112 us -> 55.6 us  [swap(): return lax.ppermute(value, axis, [(i, i ^ bit) for i in range(size)])]
    pallas_call x4, Pallas kernels: 57.4 us -> 30.8 us  [times_columns(): pl.pallas_call(lambda *refs: columns_kernel(*refs, block=block), in_specs...]
    unnamed x5 -> x13, local copies, waits for them, and re-layouts: 1 us -> 25.6 us
    ppermute x26 -> x14, starting transfers between devices: 30.4 us -> 10.2 us  [swap(): return lax.ppermute(value, axis, [(i, i ^ bit) for i in range(size)])]
    all_to_all x0 -> x1, waiting for transfers between devices: none -> 7.39 us  [sum_parts(): lax.all_to_all(jnp.broadcast_to(mine, value.shape), axis, 0, 0, tiled=True)]
    all_to_all x0 -> x1, starting transfers between devices: none -> 3.38 us  [sum_parts(): lax.all_to_all(jnp.broadcast_to(mine, value.shape), axis, 0, 0, tiled=True)]
  transfers between devices with their start and end apart: 26 -> 15, of which waited for: 26 -> 15; matrix products, arithmetic and copies ran while one was open for 0% -> 0% of each run, Pallas kernels for 0% -> 0%
where the time goes in v2:
time: 294 us; the launch traced here: 292 us
  Pallas kernels  111 us (38%)
  blocking collectives  76.3 us (26%)
  waiting for transfers between devices  62.9 us (21%)
  local copies, waits for them, and re-layouts  26.3 us (9%)
  starting transfers between devices  13.6 us (5%)
    pallas_call x4, Pallas kernels, times_rows(): pl.pallas_call(rows_kernel, grid=(rows // block,), in_specs=[pl.BlockSpec...  63.5 us
    ppermute x14, waiting for transfers between devices, swap(): return lax.ppermute(value, axis, [(i, i ^ bit) for i in range(size)])  55.6 us
    all_to_all x4, blocking collectives, sum_parts(): lax.all_to_all(value, axis, 0, 0, tiled=True)  45.2 us
    all_to_all x3, blocking collectives, sum_parts(): lax.all_to_all(jnp.broadcast_to(mine, value.shape), axis, 0, 0, tiled=True)  31.1 us
    pallas_call x4, Pallas kernels, times_columns(): pl.pallas_call(lambda *refs: columns_kernel(*refs, block=block), in_specs...  30.8 us
    unnamed x13, local copies, waits for them, and re-layouts  25.6 us
    ppermute x14, starting transfers between devices, swap(): return lax.ppermute(value, axis, [(i, i ^ bit) for i in range(size)])  10.2 us
    pallas_call x3, Pallas kernels, shards(): pl.pallas_call(head_kernel, out_shape=jax.ShapeDtypeStruct((R, columns),...  9.12 us
  transfers between devices with their start and end apart: 15, of which 15 were waited for; matrix products, arithmetic and copies ran while one was open for 0% of the time, Pallas kernels for 0%

profile of v2, /device:TPU:0, one launch (start us, length us, event | category | flops | bytes accessed | tf_op | source)
XLA Modules:
  0.0 292.5 jit_solution(15948044161623179185)
XLA Ops:
  0.7 0.9 copy-done.4
  1.5 16.5 %times_rows.4 = (f32[32,6144]{1,0:T(8,128)S(1)}, bf16[2048,6144]{1,0:T(8,128)(2,1)S(1)}) custom-call(f32[32,1024]{1,0:T(8,128)S(1)} %bitcast.1, f32[6144,1024]{1,0:T(8,128)} %a_ref.7), custom_call_target="tpu_custom_call" | custom-call | tf_op jit(solution)/shard_map/times_rows/pallas_call | solution.py:166
  18.1 0.5 collective-permute-start
  18.6 1.3 collective-permute-done
  20.0 2.9 %collective-permute-start.1 = (f32[32,3072]{1,0:T(8,128)S(1)}, f32[32,3072]{1,0:T(8,128)S(1)}, u32[]{:S(2)}, u32[]{:S(2)}) collective-permute-start(f32[32,3072]{1,0:T(8,128)S(1)} %select_add_fusion.3), channel_id=1, source_target_pairs={{0,2},{1,3},{2,0},{3,1},{4,6},{5,7},{6,4},{7,5},{8,10},{9,11},{10,... | collective-permute-start | bytes 1179656 | tf_op jit(solution)/shard_map/ppermute | solution.py:197
  23.0 9.4 %collective-permute-done.1 = f32[32,3072]{1,0:T(8,128)S(1)} collective-permute-done((f32[32,3072]{1,0:T(8,128)S(1)}, f32[32,3072]{1,0:T(8,128)S(1)}, u32[]{:S(2)}, u32[]{:S(2)}) %collective-permute-start.1) | collective-permute-done | bytes 393248 | tf_op jit(solution)/shard_map/ppermute | solution.py:197
  32.5 1.7 collective-permute-done.2
  34.3 7.7 %times_columns.4 = f32[8,40,128]{2,1,0:T(8,128)S(1)} custom-call(f32[32,6144]{1,0:T(8,128)S(1)} %pad_maximum_fusion.refs_0_, bf16[2048,6144]{1,0:T(8,128)(2,1)S(1)} %get-tuple-element.11.refs_1_), custom_call_target="tpu_custom_call" | custom-call | tf_op jit(solution)/shard_map/times_columns/pallas_call | solution.py:184
  42.1 8.3 %copy-done = bf16[2048,6144]{1,0:T(8,128)(2,1)} copy-done((bf16[2048,6144]{1,0:T(8,128)(2,1)}, bf16[2048,6144]{1,0:T(8,128)(2,1)S(1)}, u32[]{:S(2)}) %copy-start) | copy-done | bytes 25165848
  50.4 13.6 %all_to_all.40 = f32[8,40,128]{2,1,0:T(8,128)S(1)} all-to-all(f32[8,40,128]{2,1,0:T(8,128)S(1)} %times_columns.4), channel_id=1, replica_groups=mesh['space'=8,'param'=4] {'space'}, dimensions={0} | all-to-all | bytes 327680 | tf_op jit(solution)/shard_map/all_to_all | solution.py:226
  64.0 10.6 %all_to_all.41.t_ref = f32[8,40,128]{2,1,0:T(8,128)S(1)} all-to-all(f32[8,40,128]{2,1,0:T(8,128)S(1)} %broadcast_in_dim.8), channel_id=1, replica_groups=mesh['space'=8,'param'=4] {'space'}, dimensions={0} | all-to-all | bytes 327680 | tf_op jit(solution)/shard_map/all_to_all | solution.py:227
  74.6 3.0 %head.3.frame_ref = f32[32,1024]{1,0:T(8,128)S(1)} custom-call(f32[8,40,128]{2,1,0:T(8,128)S(1)} %all_to_all.41.t_ref), custom_call_target="tpu_custom_call" | custom-call | tf_op jit(solution)/shard_map/head/pallas_call | solution.py:241
  77.6 15.7 %times_rows.5 = f32[32,6144]{1,0:T(8,128)S(1)} custom-call(f32[32,1024]{1,0:T(8,128)S(1)} %head.3.frame_ref, f32[6144,1024]{1,0:T(8,128)} %a_ref.7), custom_call_target="tpu_custom_call" | custom-call | tf_op jit(solution)/shard_map/times_rows/pallas_call | solution.py:166
  93.4 1.7 collective-permute-done.3
  95.2 1.5 collective-permute-start.4
  96.8 9.7 %collective-permute-done.4 = f32[32,3072]{1,0:T(8,128)S(1)} collective-permute-done((f32[32,3072]{1,0:T(8,128)S(1)}, f32[32,3072]{1,0:T(8,128)S(1)}, u32[]{:S(2)}, u32[]{:S(2)}) %collective-permute-start.4) | collective-permute-done | bytes 393248 | tf_op jit(solution)/shard_map/ppermute | solution.py:197
  106.6 1.7 collective-permute-done.5
  108.4 7.7 %times_columns.5 = f32[8,40,128]{2,1,0:T(8,128)S(1)} custom-call(f32[32,6144]{1,0:T(8,128)S(1)} %pad_maximum_fusion.1.refs_0_, bf16[2048,6144]{1,0:T(8,128)(2,1)S(1)} %copy-done.1), custom_call_target="tpu_custom_call" | custom-call | tf_op jit(solution)/shard_map/times_columns/pallas_call | solution.py:184
  116.1 10.4 %all_to_all.42 = f32[8,40,128]{2,1,0:T(8,128)S(1)} all-to-all(f32[8,40,128]{2,1,0:T(8,128)S(1)} %times_columns.5), channel_id=1, replica_groups=mesh['space'=8,'param'=4] {'space'}, dimensions={0} | all-to-all | bytes 327680 | tf_op jit(solution)/shard_map/all_to_all | solution.py:226
  126.6 10.3 %all_to_all.43.t_ref = f32[8,40,128]{2,1,0:T(8,128)S(1)} all-to-all(f32[8,40,128]{2,1,0:T(8,128)S(1)} %broadcast_in_dim.9), channel_id=1, replica_groups=mesh['space'=8,'param'=4] {'space'}, dimensions={0} | all-to-all | bytes 327680 | tf_op jit(solution)/shard_map/all_to_all | solution.py:227
  136.9 3.0 %head.4.frame_ref = f32[32,1024]{1,0:T(8,128)S(1)} custom-call(f32[8,40,128]{2,1,0:T(8,128)S(1)} %all_to_all.43.t_ref), custom_call_target="tpu_custom_call" | custom-call | tf_op jit(solution)/shard_map/head/pallas_call | solution.py:241
  139.9 15.7 %times_rows.6 = f32[32,6144]{1,0:T(8,128)S(1)} custom-call(f32[32,1024]{1,0:T(8,128)S(1)} %head.4.frame_ref, f32[6144,1024]{1,0:T(8,128)} %a_ref.7), custom_call_target="tpu_custom_call" | custom-call | tf_op jit(solution)/shard_map/times_rows/pallas_call | solution.py:166
  155.7 1.7 collective-permute-done.6
  157.5 1.6 collective-permute-start.7
  159.1 9.7 %collective-permute-done.7 = f32[32,3072]{1,0:T(8,128)S(1)} collective-permute-done((f32[32,3072]{1,0:T(8,128)S(1)}, f32[32,3072]{1,0:T(8,128)S(1)}, u32[]{:S(2)}, u32[]{:S(2)}) %collective-permute-start.7) | collective-permute-done | bytes 393248 | tf_op jit(solution)/shard_map/ppermute | solution.py:197
  168.9 1.7 collective-permute-done.8
  170.7 8.1 %copy-done.2 = bf16[2048,6144]{1,0:T(8,128)(2,1)S(1)} copy-done((bf16[2048,6144]{1,0:T(8,128)(2,1)S(1)}, bf16[2048,6144]{1,0:T(8,128)(2,1)}, u32[]{:S(2)}) %copy-start.2) | copy-done | bytes 25165848
  178.8 7.7 %times_columns.6 = f32[8,40,128]{2,1,0:T(8,128)S(1)} custom-call(f32[32,6144]{1,0:T(8,128)S(1)} %pad_maximum_fusion.2.refs_0_, bf16[2048,6144]{1,0:T(8,128)(2,1)S(1)} %copy-done.2), custom_call_target="tpu_custom_call" | custom-call | tf_op jit(solution)/shard_map/times_columns/pallas_call | solution.py:184
  186.5 10.6 %all_to_all.44 = f32[8,40,128]{2,1,0:T(8,128)S(1)} all-to-all(f32[8,40,128]{2,1,0:T(8,128)S(1)} %times_columns.6), channel_id=1, replica_groups=mesh['space'=8,'param'=4] {'space'}, dimensions={0} | all-to-all | bytes 327680 | tf_op jit(solution)/shard_map/all_to_all | solution.py:226
  197.2 10.3 %all_to_all.45.t_ref = f32[8,40,128]{2,1,0:T(8,128)S(1)} all-to-all(f32[8,40,128]{2,1,0:T(8,128)S(1)} %broadcast_in_dim.10), channel_id=1, replica_groups=mesh['space'=8,'param'=4] {'space'}, dimensions={0} | all-to-all | bytes 327680 | tf_op jit(solution)/shard_map/all_to_all | solution.py:227
  207.5 3.0 %head.5.frame_ref = f32[32,1024]{1,0:T(8,128)S(1)} custom-call(f32[8,40,128]{2,1,0:T(8,128)S(1)} %all_to_all.45.t_ref), custom_call_target="tpu_custom_call" | custom-call | tf_op jit(solution)/shard_map/head/pallas_call | solution.py:241
  210.5 15.7 %times_rows.7 = f32[32,6144]{1,0:T(8,128)S(1)} custom-call(f32[32,1024]{1,0:T(8,128)S(1)} %head.5.frame_ref, f32[6144,1024]{1,0:T(8,128)} %a_ref.7), custom_call_target="tpu_custom_call" | custom-call | tf_op jit(solution)/shard_map/times_rows/pallas_call | solution.py:166
  226.3 1.7 collective-permute-done.9
  228.1 1.6 collective-permute-start.10
  229.7 9.7 %collective-permute-done.10 = f32[32,3072]{1,0:T(8,128)S(1)} collective-permute-done((f32[32,3072]{1,0:T(8,128)S(1)}, f32[32,3072]{1,0:T(8,128)S(1)}, u32[]{:S(2)}, u32[]{:S(2)}) %collective-permute-start.10) | collective-permute-done | bytes 393248 | tf_op jit(solution)/shard_map/ppermute | solution.py:197
  239.5 1.7 collective-permute-done.11
  241.3 8.1 %copy-done.3 = bf16[2048,6144]{1,0:T(8,128)(2,1)S(1)} copy-done((bf16[2048,6144]{1,0:T(8,128)(2,1)S(1)}, bf16[2048,6144]{1,0:T(8,128)(2,1)}, u32[]{:S(2)}) %copy-start.3) | copy-done | bytes 25165848
  249.5 7.7 %times_columns.7 = f32[8,40,128]{2,1,0:T(8,128)S(1)} custom-call(f32[32,6144]{1,0:T(8,128)S(1)} %pad_maximum_fusion.3.refs_0_.refs_1_, bf16[2048,6144]{1,0:T(8,128)(2,1)S(1)} %copy-done.3), custom_call_target="tpu_custom_call" | custom-call | tf_op jit(solution)/shard_map/times_columns/pallas_call | solution.py:184
  257.2 10.4 %all_to_all.46 = f32[8,40,128]{2,1,0:T(8,128)S(1)} all-to-all(f32[8,40,128]{2,1,0:T(8,128)S(1)} %times_columns.7), channel_id=1, replica_groups=mesh['space'=8,'param'=4] {'space'}, dimensions={0} | all-to-all | bytes 327680 | tf_op jit(solution)/shard_map/all_to_all | solution.py:226
  267.6 0.7 broadcast_in_dim.11
  268.3 3.4 %all-to-all-start.7 = ((f32[8,40,128]{2,1,0:T(8,128)}), f32[8,40,128]{2,1,0:T(8,128)S(1)}, u32[]{:S(2)}, u32[]{:S(2)}) async-start(f32[8,40,128]{2,1,0:T(8,128)} %broadcast_in_dim.11), calls=%async_computation.7 | async-start | bytes 327680 | tf_op jit(solution)/shard_map/all_to_all | solution.py:227
  271.7 0.1 copy.6.refs_2_
  271.8 7.4 %all-to-all-done.7.refs_0_ = f32[8,40,128]{2,1,0:T(8,128)S(1)} async-done(((f32[8,40,128]{2,1,0:T(8,128)}), f32[8,40,128]{2,1,0:T(8,128)S(1)}, u32[]{:S(2)}, u32[]{:S(2)}) %all-to-all-start.7) | async-done | bytes 163872 | tf_op jit(solution)/shard_map/all_to_all | solution.py:227
  279.2 4.3 %last.1 = (f32[32,6144]{1,0:T(8,128)}, f32[32,128]{1,0:T(8,128)S(1)}, f32[32,384]{1,0:T(8,128)S(1)}) custom-call(f32[8,40,128]{2,1,0:T(8,128)S(1)} %all-to-all-done.7.refs_0_, f32[32,6144]{1,0:T(8,128)S(1)} %pad_maximum_fusion.3.refs_0_.refs_1_, f32[256,32]{1,0:T(8,128)S(1)} %copy.6.refs_2_), custom_call_target="tpu_custom_call" | custom-call | tf_op jit(solution)/shard_map/last/pallas_call | solution.py:249
  283.6 1.2 collective-permute-done.12
  284.9 1.6 collective-permute-start.13
  286.4 2.6 collective-permute-done.13
  289.0 3.5 %second.1 = (f32[32,128]{1,0:T(8,128)}, f32[32,256]{1,0:T(8,128)}) custom-call(f32[32,384]{1,0:T(8,128)S(1)} %add.47.refs_0_, f32[32,128]{1,0:T(8,128)S(1)} %get-tuple-element.14.refs_1_), custom_call_target="tpu_custom_call" | custom-call | tf_op jit(solution)/shard_map/second/pallas_call | solution.py:261
  (45 shorter events, 1.8 us)
Async XLA Ops:
  0.6 0.9 copy-start.4
  18.1 1.9 collective-permute-start
  20.0 12.3 %collective-permute-start.1 = (f32[32,3072]{1,0:T(8,128)S(1)}, f32[32,3072]{1,0:T(8,128)S(1)}, u32[]{:S(2)}, u32[]{:S(2)}) collective-permute-start(f32[32,3072]{1,0:T(8,128)S(1)} %select_add_fusion.3), channel_id=1, source_target_pairs={{0,2},{1,3},{2,0},{3,1},{4,6},{5,7},{6,4},{7,5},{8,10},{9,11},{10,... | collective-permute-start | bytes 1179656 | tf_op jit(solution)/shard_map/ppermute | solution.py:197
  32.4 1.8 collective-permute-start.2
  42.0 8.3 %copy-start = (bf16[2048,6144]{1,0:T(8,128)(2,1)}, bf16[2048,6144]{1,0:T(8,128)(2,1)S(1)}, u32[]{:S(2)}) copy-start(bf16[2048,6144]{1,0:T(8,128)(2,1)S(1)} %get-tuple-element.11.refs_1_) | copy-start | bytes 75497472
  64.0 44.4 %copy-start.1 = (bf16[2048,6144]{1,0:T(8,128)(2,1)S(1)}, bf16[2048,6144]{1,0:T(8,128)(2,1)}, u32[]{:S(2)}) copy-start(bf16[2048,6144]{1,0:T(8,128)(2,1)} %copy-done) | copy-start | bytes 75497472
  93.4 1.8 collective-permute-start.3
  95.2 11.2 %collective-permute-start.4 = (f32[32,3072]{1,0:T(8,128)S(1)}, f32[32,3072]{1,0:T(8,128)S(1)}, u32[]{:S(2)}, u32[]{:S(2)}) collective-permute-start(f32[32,3072]{1,0:T(8,128)S(1)} %select_add_fusion.2), channel_id=1, source_target_pairs={{0,2},{1,3},{2,0},{3,1},{4,6},{5,7},{6,4},{7,5},{8,10},{9,11},{10,... | collective-permute-start | bytes 1179656 | tf_op jit(solution)/shard_map/ppermute | solution.py:197
  106.5 1.8 collective-permute-start.5
  155.6 1.8 collective-permute-start.6
  157.5 11.2 %collective-permute-start.7 = (f32[32,3072]{1,0:T(8,128)S(1)}, f32[32,3072]{1,0:T(8,128)S(1)}, u32[]{:S(2)}, u32[]{:S(2)}) collective-permute-start(f32[32,3072]{1,0:T(8,128)S(1)} %select_add_fusion.1), channel_id=1, source_target_pairs={{0,2},{1,3},{2,0},{3,1},{4,6},{5,7},{6,4},{7,5},{8,10},{9,11},{10,... | collective-permute-start | bytes 1179656 | tf_op jit(solution)/shard_map/ppermute | solution.py:197
  168.8 1.8 collective-permute-start.8
  170.7 8.2 %copy-start.2 = (bf16[2048,6144]{1,0:T(8,128)(2,1)S(1)}, bf16[2048,6144]{1,0:T(8,128)(2,1)}, u32[]{:S(2)}) copy-start(bf16[2048,6144]{1,0:T(8,128)(2,1)} %copy-done) | copy-start | bytes 75497472
  210.5 61.2 %copy-start.5 = (f32[256,32]{0,1:T(8,128)S(1)}, f32[256,32]{0,1:T(8,128)}, u32[]{:S(2)}) copy-start(f32[256,32]{0,1:T(8,128)} %param.5) | copy-start | bytes 98308
  226.3 1.8 collective-permute-start.9
  228.1 11.2 %collective-permute-start.10 = (f32[32,3072]{1,0:T(8,128)S(1)}, f32[32,3072]{1,0:T(8,128)S(1)}, u32[]{:S(2)}, u32[]{:S(2)}) collective-permute-start(f32[32,3072]{1,0:T(8,128)S(1)} %select_add_fusion), channel_id=1, source_target_pairs={{0,2},{1,3},{2,0},{3,1},{4,6},{5,7},{6,4},{7,5},{8,10},{9,11},{10,... | collective-permute-start | bytes 1179656 | tf_op jit(solution)/shard_map/ppermute | solution.py:197
  239.4 1.8 collective-permute-start.11
  241.3 8.2 %copy-start.3 = (bf16[2048,6144]{1,0:T(8,128)(2,1)S(1)}, bf16[2048,6144]{1,0:T(8,128)(2,1)}, u32[]{:S(2)}) copy-start(bf16[2048,6144]{1,0:T(8,128)(2,1)} %copy-done) | copy-start | bytes 75497472
  268.3 10.9 %all-to-all-start.7 = ((f32[8,40,128]{2,1,0:T(8,128)}), f32[8,40,128]{2,1,0:T(8,128)S(1)}, u32[]{:S(2)}, u32[]{:S(2)}) async-start(f32[8,40,128]{2,1,0:T(8,128)} %broadcast_in_dim.11), calls=%async_computation.7 | async-start | bytes 327680 | tf_op jit(solution)/shard_map/all_to_all | solution.py:227
  283.5 1.3 collective-permute-start.12
  284.9 4.2 %collective-permute-start.13 = (f32[32,384]{1,0:T(8,128)S(1)}, f32[32,384]{1,0:T(8,128)S(1)}, u32[]{:S(2)}, u32[]{:S(2)}) collective-permute-start(f32[32,384]{1,0:T(8,128)S(1)} %add.46), channel_id=1, source_target_pairs={{0,2},{1,3},{2,0},{3,1},{4,6},{5,7},{6,4},{7,5},{8,10},{9,11},{10,... | collective-permute-start | bytes 147464 | tf_op jit(solution)/shard_map/ppermute | solution.py:197
